TPU v7x, 256 devices: a whole 4x4x8 slice. The times are simulated.
256 devices in a mesh: seed: 4 (over x), fsdp: 8 (over y, core), seq: 8 (over z).
Axes of the slice: x: 4, y: 4, z: 8, core: 2. Of those that a mesh axis runs over, the one named last changes fastest.
Arguments:
- mel_frames: bfloat16 [8, 32768, 80], P('fsdp', 'seq'), may hold values from -6 to 6
- lengths: int32 [8], P('fsdp'), may hold values from 1 to 8192, 40960 in all
- targets: int32 [8, 8192], P('fsdp', 'seq'), may hold values from 0 to 511
- frame_mask: int32 [8, 8192], P('fsdp', 'seq'), may hold values 0 or 1
- stem_weight: bfloat16 [4, 640, 1536], P('seed'), may hold values from -0.25 to 0.25
- conv_in_weight: bfloat16 [4, 1536, 1536], P('seed', ('fsdp', 'seq')), may hold values from -0.15625 to 0.15625
- conv_out_weight: bfloat16 [4, 768, 1536], P('seed', ('fsdp', 'seq')), may hold values from -0.21875 to 0.21875
- depth_weight: bfloat16 [4, 31, 768], P('seed'), may hold values from -1 to 1
- head_weight: bfloat16 [4, 1536, 512], P('seed', ('fsdp', 'seq')), may hold values from -80 to 80
- norm_gain: float32 [4, 2, 1536], P('seed'), may hold values from 0.5 to 1.5
Outputs:
- frame_error: float32 [8, 8192], P('fsdp', 'seq')
- utt_score: float32 [8], P('fsdp')
Inputs may be any that keep to these rules, and one draw needn't show every extreme that they name: `lengths`: some utterance has exactly 8192 valid frames.
All inputs are finite; a program needn't handle non-finite values. No bound on the sum of `lengths` or of `frame_mask` on one device may be relied on, other than what follows from the above.
Results may differ from a plain program's by a relative error of at most 0.0022.
Values may be sent and summed in bfloat16 or wider, within the bound.
A program may use at most 64 MiB of HBM per device.

v0:
```python
import jax
import jax.numpy as jnp
from jax import lax
from jax.sharding import PartitionSpec as P


def from_behind(x, axis, by):
    count = lax.axis_size(axis)
    pairs = [(i, i + by) for i in range(count) if 0 <= i + by < count]
    return lax.ppermute(x, axis, pairs)


def extended(x, sides, width):
    for axis, dim in sides:
        count, length = (lax.axis_size(axis), x.shape[dim])
        up = [(i, (i + 1) % count) for i in range(count - 1)]
        down = [(j, i) for i, j in up]
        last = lax.slice_in_dim(x, length - width, length, axis=dim)
        first = lax.slice_in_dim(x, 0, width, axis=dim)
        before = lax.ppermute(last, axis, up)
        after = lax.ppermute(first, axis, down)
        x = jnp.concatenate([before, x, after], axis=dim)
    return x


def layer_norm(values, gain_row):
    row_mean = jnp.mean(values, axis=-1, keepdims=True)
    centred = values - row_mean
    row_var = jnp.mean(centred * centred, axis=-1, keepdims=True)
    return (centred * lax.rsqrt(row_var + 1e-05) * gain_row).astype(jnp.bfloat16)


def block_product(left_rows, right_matrix):
    return jnp.dot(left_rows, right_matrix, preferred_element_type=jnp.float32)


def row_product(activations, shard_piece):
    return block_product(activations, shard_piece[0])


def body(
    mel_frames,
    lengths,
    targets,
    frame_mask,
    stem_weight,
    conv_in_weight,
    conv_out_weight,
    depth_weight,
    head_weight,
    norm_gain,
):
    frame_rows = targets.shape[1]
    blocks = mel_frames[0].reshape(frame_rows, -1)
    next_block = from_behind(blocks[:1], "seq", -1)
    following = jnp.concatenate([blocks[1:], next_block], 0)
    half_width = blocks.shape[1]
    stem_matrix = stem_weight[0]
    stem_out = (
        jnp.dot(blocks, stem_matrix[:half_width], preferred_element_type=jnp.float32)
        + jnp.dot(following, stem_matrix[half_width:], preferred_element_type=jnp.float32)
    ).astype(jnp.bfloat16)
    offset = lax.axis_index("seq") * frame_rows
    length = lengths[0]
    positions = offset + jnp.arange(frame_rows, dtype=jnp.int32)
    frame_live = positions < length
    gain_rows = norm_gain[0]
    normed_one = layer_norm(stem_out.astype(jnp.float32), gain_rows[0])
    tap_count = depth_weight.shape[1]
    channels = depth_weight.shape[2]
    halo_width = tap_count // 2
    mixed_rows = row_product(
        normed_one, lax.all_gather(conv_in_weight, ("fsdp", "seq"), axis=1, tiled=True)
    )
    input_positions = offset + jnp.arange(normed_one.shape[0], dtype=jnp.int32)
    input_live = jnp.logical_and(input_positions >= 0, input_positions < length)
    gated_rows = (
        mixed_rows[:, :channels]
        * jax.nn.sigmoid(mixed_rows[:, channels:])
        * input_live[:, None].astype(jnp.float32)
    ).astype(jnp.bfloat16)
    padded = extended(gated_rows, (("seq", 0),), halo_width)
    depthwise = jnp.zeros((frame_rows, channels), jnp.float32)
    for tap_index in range(tap_count):
        depthwise = depthwise + padded[tap_index : tap_index + frame_rows].astype(
            jnp.float32
        ) * depth_weight[0, tap_index].astype(jnp.float32)
    swished = jax.nn.silu(depthwise).astype(jnp.bfloat16)
    conv_proj = row_product(
        swished, lax.all_gather(conv_out_weight, ("fsdp", "seq"), axis=1, tiled=True)
    )
    after_conv = stem_out.astype(jnp.float32) + conv_proj
    normed_two = layer_norm(after_conv, gain_rows[1])
    logits = row_product(
        normed_two, lax.all_gather(head_weight, ("fsdp", "seq"), axis=1, tiled=True)
    )
    posterior = jax.nn.softmax(logits, axis=-1)
    vocab_size = logits.shape[1]
    onehot = (jnp.arange(vocab_size, dtype=jnp.int32)[None, :] == targets[0][:, None]).astype(
        jnp.float32
    )
    differ = posterior - onehot
    frame_err = (
        jnp.sqrt(jnp.sum(differ * differ, axis=-1))
        * frame_live.astype(jnp.float32)
        * frame_mask[0].astype(jnp.float32)
    )
    seed_count = lax.axis_size("seed")
    frame_error = lax.psum(frame_err, "seed") / jnp.float32(seed_count)
    numerator = lax.psum(jnp.sum(frame_error), "seq")
    utt_score = numerator / length.astype(jnp.float32)
    return (frame_error[None, :], utt_score.reshape(1))


def solution(mesh):
    in_specs = (
        P("fsdp", "seq", None),
        P("fsdp"),
        P("fsdp", "seq"),
        P("fsdp", "seq"),
        P("seed", None, None),
        P("seed", ("fsdp", "seq"), None),
        P("seed", ("fsdp", "seq"), None),
        P("seed", None, None),
        P("seed", ("fsdp", "seq"), None),
        P("seed", None, None),
    )
    out_specs = (P("fsdp", "seq"), P("fsdp"))
    return jax.shard_map(body, mesh=mesh, in_specs=in_specs, out_specs=out_specs, check_vma=False)
```

profile of v0, /device:TPU:1, one launch (start us, length us, event | category | flops | bytes accessed | tf_op | source)
XLA Modules:
  0.0 287.9 jit_solution(8486558325888110013)
XLA Ops:
  7.2 0.0 copy-start.3
  7.2 0.0 all-gather.4.cloned.1.call-start
  7.2 0.7 all-gather.4.cloned.1.call-update
  7.9 0.0 all-gather.6.cloned.1.call-start
  8.0 1.5 copy.22
  9.4 0.0 all-gather.6.cloned.1.call-update
  9.5 0.0 all-gather.8.cloned.1.call-start
  9.5 0.7 slice.261
  10.2 0.1 copy.21
  10.3 0.1 slice.262
  10.4 1.3 collective-permute-start
  11.7 0.0 all-gather.8.cloned.1.call-update
  11.7 1.6 copy.19
  13.3 1.4 convert_reduce_fusion.31
  14.8 0.7 reshape_squeeze.3
  15.4 0.0 copy-done.3
  16.1 0.0 copy-start
  16.2 5.7 %fusion.54 = f32[1024,1536]{1,0:T(8,128)} fusion(bf16[1024,320]{1,0:T(8,128)(2,1)S(1)} %reshape_squeeze.3, bf16[1,640,1536]{2,1,0:T(8,128)(2,1)} %param.14), kind=kOutput, calls=%fused_computation.110 | convolution fusion | flops 1006632960 | bytes 7929856 | tf_op jit(solution)/shard_map/dot_general | solution.py:60
  21.9 0.0 copy-done
  21.9 0.2 slice.259
  22.1 0.6 copy.20
  22.8 1.6 slice.260
  24.4 0.0 collective-permute-done
  24.4 5.2 %convert_reduce_fusion = (f32[1024]{0:T(1024)S(1)}, bf16[1024,1536]{1,0:T(8,128)(2,1)S(1)}) fusion(f32[1024,1536]{1,0:T(8,128)} %fusion.54, bf16[1,640,1536]{2,1,0:T(8,128)(2,1)} %param.14, bf16[1,320]{1,0:T(2,128)(2,1)S(1)} %collective-permute-done, bf16[1023,320]{1,0:T(8,128)(2,1)} %slice.260), kind=kOutput, calls=%fused_computation.2 | convolution fusion | flops 1014234112 | bytes 11211392 | tf_op jit(solution)/shard_map/dot_general | solution.py:61
  29.6 1.0 fusion.2
  30.6 63.9 %all-gather.4.cloned.1.call-done = bf16[1,1536,1536]{2,1,0:T(8,128)(2,1)} async-done(((bf16[1,24,1536]{2,1,0:T(8,128)(2,1)}), bf16[1,1536,1536]{2,1,0:T(8,128)(2,1)}) %all-gather.4.cloned.1.call-update) | async-done | bytes 4718608 | tf_op jit(solution)/shard_map/all_gather | solution.py:73
  94.6 7.2 %fusion.5 = f32[1024,1536]{1,0:T(8,128)S(1)} fusion(bf16[1,1536,1536]{2,1,0:T(8,128)(2,1)} %all-gather.4.cloned.1.call-done, bf16[1024,1536]{1,0:T(8,128)(2,1)S(1)} %get-tuple-element.40, f32[1536]{0:T(1024)S(1)} %get-tuple-element.34, f32[1024]{0:T(1024)S(1)} %add_rsqrt_fusion.1, f32[1024]{0:T(1024)S(1)} %broadcast_multiply_fusion.2), kind=kOutput, calls=%fused_computation.39 | convolution fusion | flops 4839702528 | bytes 14170112 | tf_op jit(solution)/shard_map/dot_general | solution.py:34
  101.8 0.0 copy-start.2
  101.8 0.0 copy-start.5
  101.8 0.8 fusion.20
  102.7 0.0 copy-start.1
  102.7 1.1 copy-done.1
  103.8 2.2 collective-permute-start.1
  106.0 1.5 collective-permute-start.2
  107.5 0.0 copy-done.2
  107.5 0.1 convert_reduce_fusion.30
  107.6 0.0 copy-done.5
  107.6 66.5 %all-gather.6.cloned.1.call-done = bf16[1,768,1536]{2,0,1:T(2,128)(2,1)} async-done(((bf16[1,12,1536]{2,0,1:T(2,128)(2,1)}), bf16[1,768,1536]{2,0,1:T(2,128)(2,1)}) %all-gather.6.cloned.1.call-update) | async-done | bytes 2359312 | tf_op jit(solution)/shard_map/all_gather | solution.py:90
  174.1 0.0 collective-permute-done.1
  174.1 0.0 collective-permute-done.2
  174.1 48.2 %fusion.70 = (f32[1024]{0:T(1024)S(1)}, f32[1024,1536]{1,0:T(8,128)}) fusion(bf16[1,768,1536]{2,0,1:T(2,128)(2,1)} %all-gather.6.cloned.1.call-done, bf16[1024,768]{1,0:T(8,128)(2,1)} %copy-done.1, bf16[15,768]{1,0:T(8,128)(2,1)S(1)} %collective-permute-done.2, bf16[15,768]{1,0:T(8,128)(2,1)S(1)} %collective-permute-done.1, ...), kind=kOutput, calls=%fused_computation.166 | convolution fusion | flops 2567699456 | bytes 13514752 | tf_op jit(solution)/shard_map/dot_general | solution.py:34
  222.3 3.5 %multiply_reduce_fusion = f32[1024]{0:T(1024)S(1)} fusion(f32[1024,1536]{1,0:T(8,128)} %get-tuple-element.42, f32[1024]{0:T(1024)S(1)} %broadcast_multiply_fusion.1), kind=kLoop, calls=%fused_computation.37 | loop fusion | flops 4717568 | bytes 6299648 | tf_op jit(solution)/shard_map/reduce_sum | solution.py:29
  225.8 25.2 %all-gather.8.cloned.1.call-done = bf16[1,1536,512]{2,1,0:T(8,128)(2,1)} async-done(((bf16[1,24,512]{2,1,0:T(8,128)(2,1)}), bf16[1,1536,512]{2,1,0:T(8,128)(2,1)}) %all-gather.8.cloned.1.call-update) | async-done | bytes 1572880 | tf_op jit(solution)/shard_map/all_gather | solution.py:95
  251.0 0.0 copy-start.4
  251.0 5.0 %fusion.71 = (f32[1024]{0:T(1024)S(1)}, f32[1024,512]{0,1:T(8,128)S(1)}) fusion(bf16[1,1536,512]{2,1,0:T(8,128)(2,1)} %all-gather.8.cloned.1.call-done, f32[1024,1536]{1,0:T(8,128)} %get-tuple-element.42, f32[1536]{0:T(1024)S(1)} %get-tuple-element.33, f32[1024]{0:T(1024)S(1)} %add_rsqrt_fusion, f32[1024]{0:T(1024)S(1)} %broadcast_multiply_fusion.1), kind=kOutput, calls=%fused_computation.167 | convolution fusion | flops 1617427456 | bytes 9979904 | tf_op jit(solution)/shard_map/dot_general | solution.py:34
  256.0 0.3 fusion.23
  256.4 0.0 copy-done.4
  256.4 0.7 multiply_reduce_fusion.1
  257.1 8.4 %psum.14 = f32[1024]{0:T(1024)S(1)} all-reduce(f32[1024]{0:T(1024)S(1)} %select_multiply_fusion), channel_id=1, replica_groups=mesh['seed'=4,'fsdp'=8,'seq'=8] {'seed'}, use_global_device_ids=true, to_apply=%region_7.8 | all-reduce | flops 1024 | bytes 8192 | tf_op jit(solution)/shard_map/psum | solution.py:109
  265.5 1.2 fusion.68
  266.7 12.9 %psum.15 = f32[]{:T(128)} all-reduce(f32[]{:T(128)} %get-tuple-element.37), channel_id=1, replica_groups=mesh['seed'=4,'fsdp'=8,'seq'=8] {'seq'}, use_global_device_ids=true, to_apply=%region_9.10 | all-reduce | flops 1 | bytes 8 | tf_op jit(solution)/shard_map/psum | solution.py:110
  (9 shorter events, 0.1 us)
Async XLA Ops:
  7.2 8.3 %copy-start.3 = (f32[1,2,1536]{2,1,0:T(2,128)S(1)}, f32[1,2,1536]{2,1,0:T(2,128)}, u32[]{:S(2)}) copy-start(f32[1,2,1536]{2,1,0:T(2,128)} %param.19) | copy-start | bytes 36868
  7.2 87.4 %all-gather.4.cloned.1.call-start = ((), (), s32[]{:S(2)}) async-start(), calls=%async_computation | async-start | bytes 4792320 | tf_op jit(solution)/shard_map/all_gather | solution.py:73
  7.9 166.2 %all-gather.6.cloned.1.call-start = ((), (), s32[]{:S(2)}) async-start(), calls=%async_computation.1 | async-start | bytes 4792320 | tf_op jit(solution)/shard_map/all_gather | solution.py:90
  9.5 241.5 %all-gather.8.cloned.1.call-start = ((), (), s32[]{:S(2)}) async-start(), calls=%async_computation.2 | async-start | bytes 1597440 | tf_op jit(solution)/shard_map/all_gather | solution.py:95
  10.4 14.0 %collective-permute-start = (bf16[1,320]{1,0:T(2,128)(2,1)S(1)}, bf16[1,320]{1,0:T(2,128)(2,1)S(1)}, u32[]{:S(2)}, u32[]{:S(2)}) collective-permute-start(bf16[1,320]{1,0:T(2,128)(2,1)S(1)} %slice.262), channel_id=1, source_target_pairs={{1,0},{2,1},{3,2},{4,3},{5,4},{6,5},{7,6},{9,8},{10,9},{11,10},{12... | collective-permute-start | bytes 1928 | tf_op jit(solution)/shard_map/ppermute | solution.py:10
  16.1 5.7 %copy-start = (bf16[1,4096,80]{1,2,0:T(8,128)(2,1)S(1)}, bf16[1,4096,80]{1,2,0:T(8,128)(2,1)}, u32[]{:S(2)}) copy-start(bf16[1,4096,80]{1,2,0:T(8,128)(2,1)} %param.10) | copy-start | bytes 1966084
  101.8 5.7 %copy-start.2 = (bf16[1,31,768]{2,1,0:T(8,128)(2,1)S(1)}, bf16[1,31,768]{2,1,0:T(8,128)(2,1)}, u32[]{:S(2)}) copy-start(bf16[1,31,768]{2,1,0:T(8,128)(2,1)} %param.17) | copy-start | bytes 142852
  101.8 5.8 %copy-start.5 = (s32[1,1024]{1,0:T(1,128)S(1)}, s32[1,1024]{1,0:T(1,128)}, u32[]{:S(2)}) copy-start(s32[1,1024]{1,0:T(1,128)} %param.13) | copy-start | bytes 12292
  102.7 1.1 copy-start.1
  103.8 70.3 %collective-permute-start.1 = (bf16[15,768]{1,0:T(8,128)(2,1)S(1)}, bf16[15,768]{1,0:T(8,128)(2,1)S(1)}, u32[]{:S(2)}, u32[]{:S(2)}) collective-permute-start(bf16[15,768]{1,0:T(8,128)(2,1)S(1)} %get-tuple-element.35), channel_id=1, source_target_pairs={{0,1},{1,2},{2,3},{3,4},{4,5},{5,6},{6,7},{8,9},{9,10},{10,11},{11... | collective-permute-start | bytes 69128 | tf_op jit(solution)/shard_map/ppermute | solution.py:20
  106.0 68.1 %collective-permute-start.2 = (bf16[15,768]{1,0:T(8,128)(2,1)S(1)}, bf16[15,768]{1,0:T(8,128)(2,1)S(1)}, u32[]{:S(2)}, u32[]{:S(2)}) collective-permute-start(bf16[15,768]{1,0:T(8,128)(2,1)S(1)} %get-tuple-element.36), channel_id=1, source_target_pairs={{1,0},{2,1},{3,2},{4,3},{5,4},{6,5},{7,6},{9,8},{10,9},{11,10},{12... | collective-permute-start | bytes 69128 | tf_op jit(solution)/shard_map/ppermute | solution.py:21
  251.0 5.4 %copy-start.4 = (s32[1,1024]{1,0:T(1,128)S(1)}, s32[1,1024]{1,0:T(1,128)}, u32[]{:S(2)}) copy-start(s32[1,1024]{1,0:T(1,128)} %param.12) | copy-start | bytes 12292
Sparse Core Ops, SparseCore 0:
  10.8 83.7 all-gather.3
  97.3 76.7 all-gather.5
  176.8 74.1 all-gather.7
where the time goes:
time: 291 us; the launch traced here: 288 us
  waiting for transfers between devices  156 us (54%)
  matrix products  71.4 us (25%)
  blocking collectives  21.3 us (7%)
  between operations  16.4 us (6%)
  other arithmetic  9.14 us (3%)
  local copies, waits for them, and re-layouts  8.3 us (3%)
  starting transfers between devices  5.05 us (2%)
    all_gather x1, waiting for transfers between devices, body(): lax.all_gather(conv_out_weight, ('fsdp', 'seq'), axis=1, tiled=True)  66.5 us
    all_gather x1, waiting for transfers between devices, body(): lax.all_gather(conv_in_weight, ('fsdp', 'seq'), axis=1, tiled=True)  63.9 us
    dot_general x3, matrix products, block_product(): return jnp.dot(left_rows, right_matrix, preferred_element_type=jnp.float32)  60.4 us
    all_gather x1, waiting for transfers between devices, body(): lax.all_gather(head_weight, ('fsdp', 'seq'), axis=1, tiled=True)  25.2 us
    psum x1, blocking collectives, body(): numerator = lax.psum(jnp.sum(frame_error), 'seq')  12.9 us
    psum x1, blocking collectives, body(): frame_error = lax.psum(frame_err, 'seed') / jnp.float32(seed_count)  8.42 us
  transfers between devices with their start and end apart: 6, of which 3 were waited for; matrix products, arithmetic and copies ran while one was open for 28% of the time, Pallas kernels for 0%

commit v1 on v0

v1 whole, which is shorter than its diff:
```python
import functools

import jax
import jax.numpy as jnp
from jax import lax
from jax.experimental import pallas as pl
from jax.experimental.pallas import tpu as pltpu
from jax.sharding import PartitionSpec as P

MESH = pl.DeviceIdType.MESH
F32 = jnp.float32
BF16 = jnp.bfloat16
HALO = 16
TAIL = 80
LANES = 128
GROUP = 256
GROUPS = 3
Y, CORES, Z, X = 4, 2, 8, 4


class Piece:
    def __init__(self, place, own, dst, send, recv, local, y_first, flip):
        self.place, self.own, self.dst = place, own, dst
        self.send, self.recv, self.local = send, recv, local
        self.y_first, self.flip = y_first, flip
        self.used = 0
        self.copies = []
        self.pending = []
        self.round = 0

    def remote(self, src, dst, device):
        slot = self.used
        self.used += 1
        copy = pltpu.make_async_remote_copy(
            src_ref=src,
            dst_ref=dst,
            send_sem=self.send.at[slot],
            recv_sem=self.recv.at[slot],
            device_id=device,
            device_id_type=MESH,
        )
        copy.start()
        self.copies.append(copy)
        self.pending.append(copy)

    def at_z(self, by):
        x, y, c, z = self.place
        return (x, y * CORES + c, lax.rem(z + by + Z, Z))

    def at_y(self, by):
        x, y, c, z = self.place
        return (x, lax.rem(y + by + Y, Y) * CORES + c, z)

    def z_step(self, step):
        x, y, c, z = self.place
        for sign in (1, -1):
            if step == 4 and sign == (1 if self.flip else -1):
                continue
            owner = lax.rem(z - sign * (step - 1) + Z, Z)
            if self.y_first:
                block = self.dst.at[:, c, owner]
                self.remote(block, block, self.at_z(sign))
            else:
                block = self.dst.at[y, c, owner]
                self.remote(self.own if step == 1 else block, block, self.at_z(sign))

    def y_step(self):
        x, y, c, z = self.place
        block = self.dst.at[y, c, z] if self.y_first else self.dst.at[y, c]
        for by in (1, 3, 2):
            self.remote(self.own if self.y_first else block, block, self.at_y(by))

    def arrived(self):
        for copy in self.pending:
            copy.wait_recv()
        self.pending = []

    def step(self):
        x, y, c, z = self.place
        now = self.round
        self.round += 1
        if now == 0:
            keep = pltpu.make_async_copy(self.own, self.dst.at[y, c, z], self.local)
            if self.y_first:
                self.y_step()
            else:
                self.z_step(1)
            keep.start()
            self.keep = keep
            return
        self.arrived()
        if now == 1:
            self.keep.wait()
        if now <= 4:
            if self.y_first:
                self.z_step(now)
            elif now <= 3:
                self.z_step(now + 1)
            else:
                self.y_step()
        elif now == 5:
            block = self.dst.at[:, c]
            self.remote(block, block, (x, y * CORES + 1 - c, z))

    def finish(self):
        for copy in self.copies:
            copy.wait_send()


def normalised(values, gain_row):
    row_mean = jnp.mean(values, axis=-1, keepdims=True)
    centred = values - row_mean
    row_var = jnp.mean(centred * centred, axis=-1, keepdims=True)
    return (centred * lax.rsqrt(row_var + 1e-05) * gain_row).astype(BF16)


def dot(left, right):
    return jnp.dot(left, right, preferred_element_type=F32)


def kernel(
    rows,
    taps,
    lengths_ref,
    targets_ref,
    mask_ref,
    gain_ref,
    depth_ref,
    mel_hbm,
    stem_hbm,
    gate_hbm,
    back_hbm,
    head_hbm,
    error_ref,
    score_ref,
    mel_bf,
    mel_f32,
    stem_w,
    gate_a,
    gate_b,
    back_a,
    back_b,
    head_a,
    head_b,
    back_w,
    stem_out,
    normed,
    gated,
    swished,
    tap_rows,
    square,
    error_cols,
    seed_parts,
    seq_parts,
    send_sem,
    recv_sem,
    local_sem,
    mel_send,
    mel_recv,
    out_send,
    out_recv,
):
    x = lax.axis_index("seed")
    fsdp = lax.axis_index("fsdp")
    y, c = fsdp // CORES, lax.rem(fsdp, CORES)
    z = lax.axis_index("seq")
    place = (x, y, c, z)
    wide = rows + 2 * HALO
    channels = GROUP * GROUPS

    barrier = pltpu.get_barrier_semaphore()
    peers = [(x, fsdp, lax.rem(z + d, Z)) for d in range(1, Z)]
    peers += [(x, lax.rem(y + d, Y) * CORES + c, z) for d in range(1, Y)]
    peers += [(lax.rem(x + d, X), fsdp, z) for d in range(1, X)]
    peers += [(x, y * CORES + 1 - c, z)]
    for peer in peers:
        pl.semaphore_signal(barrier, inc=1, device_id=peer, device_id_type=MESH)

    mel_rows = 4 * rows
    loads = [
        pltpu.make_async_copy(mel_hbm.at[0], mel_bf.at[pl.ds(4 * HALO, mel_rows)], local_sem.at[10]),
        pltpu.make_async_copy(stem_hbm.at[0], stem_w, local_sem.at[11]),
    ]
    for load in loads:
        load.start()

    specs = []
    for group in range(GROUPS):
        specs.append((gate_hbm, GROUP * group, GROUP, gate_a.at[group], False))
        specs.append((gate_hbm, channels + GROUP * group, GROUP, gate_b.at[group], True))
    half = back_hbm.shape[2] // 2
    specs.append((back_hbm, 0, half, back_a, False))
    specs.append((back_hbm, half, half, back_b, True))
    quarter = head_hbm.shape[2] // 2
    specs.append((head_hbm, 0, quarter, head_a, False))
    specs.append((head_hbm, quarter, quarter, head_b, True))
    pieces = []
    for index, (source, start, width, dst, y_first) in enumerate(specs):
        own = source.at[0, :, pl.ds(start, width)]
        pieces.append(
            Piece(place, own, dst, send_sem.at[index], recv_sem.at[index], local_sem.at[index], y_first, index % 4 >= 2)
        )
    starts = (0, 0, 1, 1, 2, 2, 3, 3, 4, 4)

    def comm(now):
        for piece, start in zip(pieces, starts):
            if start <= now <= start + 6:
                piece.step()

    pl.semaphore_wait(barrier, len(peers))
    comm(0)
    halo = [
        pltpu.make_async_remote_copy(
            src_ref=mel_hbm.at[0, pl.ds(mel_rows - 4 * HALO, 4 * HALO)],
            dst_ref=mel_bf.at[pl.ds(0, 4 * HALO)],
            send_sem=mel_send.at[0],
            recv_sem=mel_recv.at[0],
            device_id=(x, fsdp, lax.rem(z + 1, Z)),
            device_id_type=MESH,
        ),
        pltpu.make_async_remote_copy(
            src_ref=mel_hbm.at[0, pl.ds(0, TAIL)],
            dst_ref=mel_bf.at[pl.ds(4 * HALO + mel_rows, TAIL)],
            send_sem=mel_send.at[1],
            recv_sem=mel_recv.at[1],
            device_id=(x, fsdp, lax.rem(z + Z - 1, Z)),
            device_id_type=MESH,
        ),
    ]
    for copy in halo:
        copy.start()

    length = lengths_ref[0]
    tap_rows[...] = jnp.zeros_like(tap_rows)
    tap_rows[1 : 1 + taps, :] = depth_ref[0].astype(F32)
    square[...] = jnp.zeros_like(square)
    blocks = rows // LANES
    for b in range(blocks):
        square[b : b + 1, :] = targets_ref[0:1, b * LANES : (b + 1) * LANES].astype(F32)
    square[...] = square[...].T

    for load in loads:
        load.wait()
    for copy in halo:
        copy.wait_recv()
    comm(1)

    mel_f32[: 4 * HALO + mel_rows, :] = mel_bf[: 4 * HALO + mel_rows, :].astype(F32)
    more = (z < Z - 1).astype(F32)
    mel_f32[4 * HALO + mel_rows :, :] = mel_bf[4 * HALO + mel_rows :, :].astype(F32) * more
    tall = wide // 3

    def stem(part):
        r0 = part * tall
        window = [mel_f32[pl.ds(4 * r0 + i, tall, stride=4), :] for i in range(8)]
        frames = jnp.concatenate(window, axis=1).astype(BF16)
        out = dot(frames, stem_w[...]).astype(BF16)
        stem_out[r0 : r0 + tall, :] = out
        normed[r0 : r0 + tall, :] = normalised(out.astype(F32), gain_ref[0, 0:1, :])

    for part in range(3):
        stem(part)
        comm(2 + part)
    comm(5)
    comm(6)

    def gate(group):
        @pl.loop(0, 3)
        def _(part):
            r0 = pl.multiple_of(part * tall, 16)
            left = normed[pl.ds(r0, tall), :]
            value = dot(left, gate_a[group].reshape(-1, GROUP))
            control = dot(left, gate_b[group].reshape(-1, GROUP))
            position = z * rows - HALO + r0 + lax.broadcasted_iota(jnp.int32, (tall, 1), 0)
            live = jnp.where((position >= 0) & (position < length), 1.0, 0.0).astype(F32)
            result = (value * jax.nn.sigmoid(control) * live).astype(BF16).astype(F32)
            for k in range(GROUP // LANES):
                gated[k, pl.ds(r0, tall), :] = result[:, k * LANES : (k + 1) * LANES]

    def depthwise(group, first, last):
        size = 64

        @pl.loop(first, last)
        def _(part):
            r0 = pl.multiple_of(part * size, size)
            for k in range(GROUP // LANES):
                column = group * GROUP + k * LANES
                around = gated[k, pl.ds(r0, size + 32), :]
                total = jnp.zeros((size, LANES), F32)
                for s in range(8):
                    partial = None
                    for a in range(4):
                        if a == 0 and s == 0:
                            continue
                        term = around[8 * a : 8 * a + size + 8] * tap_rows[8 * a + s : 8 * a + s + 1, column : column + LANES]
                        partial = term if partial is None else partial + term
                    if s:
                        partial = pltpu.roll(partial, size + 8 - s, 0)
                    total = total + partial[:size]
                swished[pl.ds(r0, size), column : column + LANES] = jax.nn.silu(total).astype(BF16)

    steps = rows // 64
    gate(0)
    comm(7)
    depthwise(0, 0, steps)
    gate(1)
    comm(8)
    depthwise(1, 0, steps)
    gate(2)
    comm(9)
    depthwise(2, 0, steps // 2)
    comm(10)
    depthwise(2, steps // 2, steps)

    @pl.loop(0, 16)
    def _(part):
        r0 = pl.multiple_of(part * 48, 48)
        flat_a = back_a.at[part // 4, lax.rem(part // 2, 2), pl.ds(lax.rem(part, 2) * 4, 4)]
        flat_b = back_b.at[part // 4, lax.rem(part // 2, 2), pl.ds(lax.rem(part, 2) * 4, 4)]
        back_w[pl.ds(r0, 48), :half] = flat_a[...].astype(F32).reshape(48, half).astype(BF16)
        back_w[pl.ds(r0, 48), half:] = flat_b[...].astype(F32).reshape(48, half).astype(BF16)

    error_cols[...] = jnp.zeros_like(error_cols)
    size = 2 * LANES
    vocab = 2 * quarter

    @pl.loop(0, rows // size)
    def _(part):
        r0 = pl.multiple_of(part * size, size)
        after = stem_out[pl.ds(r0 + HALO, size), :].astype(F32) + dot(swished[pl.ds(r0, size), :], back_w[...])
        second = normalised(after, gain_ref[0, 1:2, :])
        logits = jnp.concatenate(
            [dot(second, head_a[...].reshape(-1, quarter)), dot(second, head_b[...].reshape(-1, quarter))], axis=1
        )
        top = jnp.max(logits, axis=-1, keepdims=True)
        weight = jnp.exp(logits - top)
        posterior = weight * (1.0 / jnp.sum(weight, axis=-1, keepdims=True))
        token = lax.broadcasted_iota(jnp.int32, (LANES, vocab), 1).astype(F32)
        lane = lax.broadcasted_iota(jnp.int32, (LANES, LANES), 1)
        for k in range(2):
            here = lane == 2 * part + k
            target = jnp.sum(jnp.where(here, square[...], 0.0), axis=1, keepdims=True)
            onehot = jnp.where(token == target, 1.0, 0.0)
            differ = posterior[k * LANES : (k + 1) * LANES] - onehot
            norm = jnp.sqrt(jnp.sum(differ * differ, axis=-1, keepdims=True))
            error_cols[...] = jnp.where(here, norm, error_cols[...])

    block = lax.broadcasted_iota(jnp.int32, (blocks, LANES), 0)
    position = z * rows + block * LANES + lax.broadcasted_iota(jnp.int32, (blocks, LANES), 1)
    for b in range(blocks):
        square[b : b + 1, :] = mask_ref[0:1, b * LANES : (b + 1) * LANES].astype(F32)
    own = error_cols[...].T[:blocks] * jnp.where(position < length, 1.0, 0.0) * square[:blocks, :]
    seed_parts[x] = own
    sums = [
        pltpu.make_async_remote_copy(
            src_ref=seed_parts.at[x],
            dst_ref=seed_parts.at[x],
            send_sem=out_send.at[d],
            recv_sem=out_recv.at[d],
            device_id=(lax.rem(x + d, X), fsdp, z),
            device_id_type=MESH,
        )
        for d in range(1, X)
    ]
    for copy in sums:
        copy.start()
    for copy in sums:
        copy.wait()
    frame_error = (seed_parts[0] + seed_parts[1] + seed_parts[2] + seed_parts[3]) / 4.0
    for b in range(blocks):
        error_ref[0:1, b * LANES : (b + 1) * LANES] = frame_error[b : b + 1]
    seq_parts[z] = frame_error
    shares = [
        pltpu.make_async_remote_copy(
            src_ref=seq_parts.at[z],
            dst_ref=seq_parts.at[z],
            send_sem=out_send.at[X + d],
            recv_sem=out_recv.at[X + d],
            device_id=(x, fsdp, lax.rem(z + d, Z)),
            device_id_type=MESH,
        )
        for d in range(1, Z)
    ]
    for copy in shares:
        copy.start()
    for copy in shares:
        copy.wait()
    total = seq_parts[0]
    for k in range(1, Z):
        total = total + seq_parts[k]
    numerator = jnp.sum(jnp.sum(total, axis=1, keepdims=True), axis=0, keepdims=True)
    score_ref[...] = numerator / jnp.full((1, 1), length, jnp.int32).astype(F32)

    for copy in halo:
        copy.wait_send()
    for piece in pieces:
        piece.finish()


def body(mel, lengths, targets, mask, stem_weight, gate_weight, back_weight, depth_weight, head_weight, gain):
    rows = targets.shape[1]
    taps, channels = depth_weight.shape[1:]
    width = stem_weight.shape[2]
    wide = rows + 2 * HALO
    mels = mel.shape[2]
    mel_rows = 4 * HALO + mel.shape[1] + TAIL
    deep, thin = gate_weight.shape[1], back_weight.shape[1]
    vocab = head_weight.shape[2]
    vmem = pl.BlockSpec(memory_space=pltpu.VMEM)
    hbm = pl.BlockSpec(memory_space=pl.ANY)
    share = (Y, CORES, Z)
    blocks = rows // LANES
    flops = 2 * wide * width * (stem_weight.shape[1] + 2 * channels) + 2 * rows * width * (channels + vocab)
    error, score = pl.pallas_call(
        functools.partial(kernel, rows, taps),
        out_shape=(jax.ShapeDtypeStruct((1, rows), F32), jax.ShapeDtypeStruct((1, 1), F32)),
        in_specs=[pl.BlockSpec(memory_space=pltpu.SMEM)] + [vmem] * 4 + [hbm] * 5,
        out_specs=(vmem, vmem),
        scratch_shapes=[
            pltpu.VMEM((mel_rows, mels), BF16),
            pltpu.VMEM((mel_rows, mels), F32),
            pltpu.VMEM(stem_weight.shape[1:], BF16),
            pltpu.VMEM((GROUPS,) + share + (deep, GROUP), BF16),
            pltpu.VMEM((GROUPS,) + share + (deep, GROUP), BF16),
            pltpu.VMEM(share + (thin, width // 2), BF16),
            pltpu.VMEM(share + (thin, width // 2), BF16),
            pltpu.VMEM(share + (deep, vocab // 2), BF16),
            pltpu.VMEM(share + (deep, vocab // 2), BF16),
            pltpu.VMEM((channels, width), BF16),
            pltpu.VMEM((wide, width), BF16),
            pltpu.VMEM((wide, width), BF16),
            pltpu.VMEM((GROUP // LANES, wide, LANES), F32),
            pltpu.VMEM((rows, channels), BF16),
            pltpu.VMEM((32, channels), F32),
            pltpu.VMEM((LANES, LANES), F32),
            pltpu.VMEM((LANES, LANES), F32),
            pltpu.VMEM((X, blocks, LANES), F32),
            pltpu.VMEM((Z, blocks, LANES), F32),
            pltpu.SemaphoreType.DMA((10, 11)),
            pltpu.SemaphoreType.DMA((10, 11)),
            pltpu.SemaphoreType.DMA((12,)),
            pltpu.SemaphoreType.DMA((2,)),
            pltpu.SemaphoreType.DMA((2,)),
            pltpu.SemaphoreType.DMA((X + Z,)),
            pltpu.SemaphoreType.DMA((X + Z,)),
        ],
        compiler_params=pltpu.CompilerParams(
            collective_id=0, has_side_effects=True, vmem_limit_bytes=52 << 20
        ),
        cost_estimate=pl.CostEstimate(flops=flops, bytes_accessed=20 << 20, transcendentals=4 << 20),
        name="el2n_scores",
    )(lengths, targets, mask, gain, depth_weight, mel, stem_weight, gate_weight, back_weight, head_weight)
    return error, score.reshape(1)


def solution(mesh):
    in_specs = (
        P("fsdp", "seq", None),
        P("fsdp"),
        P("fsdp", "seq"),
        P("fsdp", "seq"),
        P("seed", None, None),
        P("seed", ("fsdp", "seq"), None),
        P("seed", ("fsdp", "seq"), None),
        P("seed", None, None),
        P("seed", ("fsdp", "seq"), None),
        P("seed", None, None),
    )
    out_specs = (P("fsdp", "seq"), P("fsdp"))
    return jax.shard_map(body, mesh=mesh, in_specs=in_specs, out_specs=out_specs, check_vma=False)
```

time: 291 us -> 93.5 us (0.32)
  waiting for transfers between devices: 156 us -> 0 us
  Pallas kernels: 0 us -> 82.6 us
  matrix products: 71.4 us -> 0 us
  blocking collectives: 21.3 us -> 0 us
  between operations: 16.4 us -> 3 us
  other arithmetic: 9.14 us -> 0 us
  starting transfers between devices: 5.05 us -> 0 us
    all_gather x3 -> x0, waiting for transfers between devices: 156 us -> none  [the longest x1 66.5 us: body(): lax.all_gather(conv_out_weight, ('fsdp', 'seq'), axis=1, tiled=True)]
    pallas_call x0 -> x1, Pallas kernels: none -> 82.6 us  [body(): pl.pallas_call(functools.partial(kernel, rows, taps), out_shape=(jax.Shap...]
    dot_general x5 -> x0, matrix products: 71.4 us -> none  [the longest x3 60.4 us: block_product(): return jnp.dot(left_rows, right_matrix, preferred_element_type=jnp.float32)]
    psum x2 -> x0, blocking collectives: 21.3 us -> none  [the longest x1 12.9 us: body(): numerator = lax.psum(jnp.sum(frame_error), 'seq')]
    reduce_sum x5 -> x0, other arithmetic: 6.71 us -> none  [the longest x2 4.51 us: layer_norm(): row_var = jnp.mean(centred * centred, axis=-1, keepdims=True)]
    ppermute x3 -> x0, starting transfers between devices: 4.94 us -> none  [the longest x1 2.17 us: extended(): before = lax.ppermute(last, axis, up)]
    slice x8 -> x0, local copies, waits for them, and re-layouts: 3.43 us -> none  [the longest x3 2.49 us: body(): following = jnp.concatenate([blocks[1:], next_block], 0)]
    unnamed x14 -> x16, local copies, waits for them, and re-layouts: 4.19 us -> 7.44 us
  transfers between devices with their start and end apart: 6 -> 0, of which waited for: 3 -> 0; matrix products, arithmetic and copies ran while one was open for 28% -> 0% of each run, Pallas kernels for 0% -> 0%
where the time goes in v1:
time: 93.5 us; the launch traced here: 93.1 us
  Pallas kernels  82.6 us (88%)
  local copies, waits for them, and re-layouts  7.44 us (8%)
  between operations  3 us (3%)
    pallas_call x1, Pallas kernels, body(): pl.pallas_call(functools.partial(kernel, rows, taps), out_shape=(jax.Shap...  82.6 us
    unnamed x16, local copies, waits for them, and re-layouts  7.44 us

profile of v1, /device:TPU:1, one launch (start us, length us, event | category | flops | bytes accessed | tf_op | source)
XLA Modules:
  0.0 93.1 jit_solution(8968295239593319822)
XLA Ops:
  1.3 1.6 %copy.12.mel_hbm = bf16[1,4096,80]{2,1,0:T(8,128)(2,1)S(1)} copy(bf16[1,4096,80]{1,2,0:T(8,128)(2,1)} %param.10) | data formatting | bytes 1310720 | tf_op args[0]
  2.8 0.0 copy-start
  2.9 0.9 copy-done
  3.7 0.0 copy-start.1
  3.7 0.8 copy-done.1
  4.5 0.0 copy-start.2
  4.5 0.8 copy-done.2
  5.3 0.0 copy-start.3
  5.3 0.7 copy-done.3
  6.1 0.0 copy-start.4
  6.1 0.7 copy-done.4
  6.8 0.0 copy-start.5
  6.8 0.7 copy-done.5
  7.5 0.0 copy-start.6
  7.5 0.7 copy-done.6
  8.1 82.6 %el2n_scores.1 = (f32[1,1024]{1,0:T(1,128)S(1)}, f32[1,1]{1,0:T(1,128)}) custom-call(s32[1]{0:T(128)S(6)} %copy.15.lengths_ref, s32[1,1024]{1,0:T(1,128)S(1)} %copy-done.5, s32[1,1024]{1,0:T(1,128)S(1)} %copy-done.6, f32[1,2,1536]{2,1,0:T(2,128)S(1)} %copy-done.4, bf16[1,31,768]{2,1,0:T(8,128)(2,1)S(1)} %copy-done.1, bf16[1,4096,80]{2,1,0:T(8,128)(2,1)S(1)} %copy.12.mel_hbm, ...), custom_call_target="tpu_custom_call" | custom-call | flops 11085545472 | bytes 20971520 | tf_op jit(solution)/shard_map/el2n_scores/pallas_call | solution.py:414
  90.8 0.6 copy.16
Async XLA Ops:
  2.8 0.9 copy-start
  3.7 0.8 copy-start.1
  4.5 0.8 copy-start.2
  5.3 0.7 copy-start.3
  6.1 0.7 copy-start.4
  6.8 0.7 copy-start.5
  7.5 0.7 copy-start.6

commit v2 on v1

--- a/solution.py
+++ b/solution.py
@@ -11,11 +11,16 @@
 F32 = jnp.float32
 BF16 = jnp.bfloat16
 HALO = 16
-TAIL = 80
 LANES = 128
 GROUP = 256
 GROUPS = 3
 Y, CORES, Z, X = 4, 2, 8, 4
+ORDER = (
+    1, 0, 3, "misc", 4, "mel0", 1, 5, 0, 3, "mel1", 4, "stem0", 1, 2, 5, "stem1", 0, "stem2", 7, 3, 4,
+    1, 2, 5, 9, 3, 0, 1, 6, 7, 2, 5, 0, 3, 1, 6, 8, 4, 9, 7, 1, "gate0", 4, 5, 3, "dw0a", 2, 8, 6, "dw0b",
+    9, 7, 3, 2, "gate1", 5, 9, 8, "dw1a", 7, "dw1b", 9, 5, 6, "gate2", 7, "dw2a", 9, 8, 6, "dw2b", 7,
+    "reloc", 9, 8, "fin",
+)
 
 
 class Piece:
@@ -51,24 +56,29 @@
         x, y, c, z = self.place
         return (x, lax.rem(y + by + Y, Y) * CORES + c, z)
 
-    def z_step(self, step):
+    def ring_step(self, step):
         x, y, c, z = self.place
         for sign in (1, -1):
-            if step == 4 and sign == (1 if self.flip else -1):
+            if step == 4 and sign == (-1 if self.flip else 1):
                 continue
-            owner = lax.rem(z - sign * (step - 1) + Z, Z)
-            if self.y_first:
-                block = self.dst.at[:, c, owner]
-                self.remote(block, block, self.at_z(sign))
-            else:
-                block = self.dst.at[y, c, owner]
-                self.remote(self.own if step == 1 else block, block, self.at_z(sign))
+            block = self.dst.at[:, c, lax.rem(z - sign * (step - 1) + Z, Z)]
+            self.remote(block, block, self.at_z(sign))
+
+    def hop(self, by, to):
+        x, y, c, z = self.place
+        block = self.dst.at[y, c, lax.rem(z + by + Z, Z)]
+        self.remote(self.own if by == 0 else block, block, self.at_z(to))
 
     def y_step(self):
         x, y, c, z = self.place
         block = self.dst.at[y, c, z] if self.y_first else self.dst.at[y, c]
-        for by in (1, 3, 2):
+        for by in (2, 1, 3):
             self.remote(self.own if self.y_first else block, block, self.at_y(by))
+
+    def across(self):
+        x, y, c, z = self.place
+        block = self.dst.at[:, c]
+        self.remote(block, block, (x, y * CORES + 1 - c, z))
 
     def arrived(self):
         for copy in self.pending:
@@ -80,27 +90,30 @@
         now = self.round
         self.round += 1
         if now == 0:
-            keep = pltpu.make_async_copy(self.own, self.dst.at[y, c, z], self.local)
+            self.keep = pltpu.make_async_copy(self.own, self.dst.at[y, c, z], self.local)
+            self.keep.start()
             if self.y_first:
                 self.y_step()
             else:
-                self.z_step(1)
-            keep.start()
-            self.keep = keep
+                for by in (2, -2, 1, -1):
+                    self.hop(0, by)
             return
         self.arrived()
         if now == 1:
             self.keep.wait()
-        if now <= 4:
-            if self.y_first:
-                self.z_step(now)
-            elif now <= 3:
-                self.z_step(now + 1)
-            else:
-                self.y_step()
-        elif now == 5:
-            block = self.dst.at[:, c]
-            self.remote(block, block, (x, y * CORES + 1 - c, z))
+        if self.y_first:
+            if now <= 4:
+                self.ring_step(now)
+            elif now == 5:
+                self.across()
+        elif now == 1:
+            self.hop(-1, 2)
+            self.hop(-2, 2)
+            self.hop(1, -2)
+        elif now == 2:
+            self.y_step()
+        elif now == 3:
+            self.across()
 
     def finish(self):
         for copy in self.copies:
@@ -122,10 +135,10 @@
     rows,
     taps,
     lengths_ref,
-    targets_ref,
-    mask_ref,
-    gain_ref,
-    depth_ref,
+    targets_hbm,
+    mask_hbm,
+    gain_hbm,
+    depth_hbm,
     mel_hbm,
     stem_hbm,
     gate_hbm,
@@ -133,6 +146,10 @@
     head_hbm,
     error_ref,
     score_ref,
+    targets_ref,
+    mask_ref,
+    gain_ref,
+    depth_ref,
     mel_bf,
     mel_f32,
     stem_w,
@@ -178,8 +195,12 @@
 
     mel_rows = 4 * rows
     loads = [
-        pltpu.make_async_copy(mel_hbm.at[0], mel_bf.at[pl.ds(4 * HALO, mel_rows)], local_sem.at[10]),
+        pltpu.make_async_copy(mel_hbm.at[0], mel_bf.at[:, pl.ds(LANES, mel_rows)], local_sem.at[10]),
         pltpu.make_async_copy(stem_hbm.at[0], stem_w, local_sem.at[11]),
+        pltpu.make_async_copy(depth_hbm, depth_ref, local_sem.at[12]),
+        pltpu.make_async_copy(targets_hbm, targets_ref, local_sem.at[13]),
+        pltpu.make_async_copy(gain_hbm, gain_ref, local_sem.at[14]),
+        pltpu.make_async_copy(mask_hbm, mask_ref, local_sem.at[15]),
     ]
     for load in loads:
         load.start()
@@ -198,71 +219,64 @@
     for index, (source, start, width, dst, y_first) in enumerate(specs):
         own = source.at[0, :, pl.ds(start, width)]
         pieces.append(
-            Piece(place, own, dst, send_sem.at[index], recv_sem.at[index], local_sem.at[index], y_first, index % 4 >= 2)
+            Piece(place, own, dst, send_sem.at[index], recv_sem.at[index], local_sem.at[index], y_first, index == 7)
         )
-    starts = (0, 0, 1, 1, 2, 2, 3, 3, 4, 4)
-
-    def comm(now):
-        for piece, start in zip(pieces, starts):
-            if start <= now <= start + 6:
-                piece.step()
-
     pl.semaphore_wait(barrier, len(peers))
-    comm(0)
     halo = [
         pltpu.make_async_remote_copy(
-            src_ref=mel_hbm.at[0, pl.ds(mel_rows - 4 * HALO, 4 * HALO)],
-            dst_ref=mel_bf.at[pl.ds(0, 4 * HALO)],
+            src_ref=mel_hbm.at[0, :, pl.ds(mel_rows - LANES, LANES)],
+            dst_ref=mel_bf.at[:, pl.ds(0, LANES)],
             send_sem=mel_send.at[0],
             recv_sem=mel_recv.at[0],
             device_id=(x, fsdp, lax.rem(z + 1, Z)),
             device_id_type=MESH,
         ),
         pltpu.make_async_remote_copy(
-            src_ref=mel_hbm.at[0, pl.ds(0, TAIL)],
-            dst_ref=mel_bf.at[pl.ds(4 * HALO + mel_rows, TAIL)],
+            src_ref=mel_hbm.at[0, :, pl.ds(0, LANES)],
+            dst_ref=mel_bf.at[:, pl.ds(LANES + mel_rows, LANES)],
             send_sem=mel_send.at[1],
             recv_sem=mel_recv.at[1],
             device_id=(x, fsdp, lax.rem(z + Z - 1, Z)),
             device_id_type=MESH,
         ),
     ]
-    for copy in halo:
-        copy.start()
-
     length = lengths_ref[0]
-    tap_rows[...] = jnp.zeros_like(tap_rows)
-    tap_rows[1 : 1 + taps, :] = depth_ref[0].astype(F32)
-    square[...] = jnp.zeros_like(square)
     blocks = rows // LANES
-    for b in range(blocks):
-        square[b : b + 1, :] = targets_ref[0:1, b * LANES : (b + 1) * LANES].astype(F32)
-    square[...] = square[...].T
-
-    for load in loads:
-        load.wait()
-    for copy in halo:
-        copy.wait_recv()
-    comm(1)
-
-    mel_f32[: 4 * HALO + mel_rows, :] = mel_bf[: 4 * HALO + mel_rows, :].astype(F32)
-    more = (z < Z - 1).astype(F32)
-    mel_f32[4 * HALO + mel_rows :, :] = mel_bf[4 * HALO + mel_rows :, :].astype(F32) * more
+
+    def small():
+        for load in loads:
+            load.wait()
+        tap_rows[...] = jnp.zeros_like(tap_rows)
+        tap_rows[1 : 1 + taps, :] = depth_ref[0].astype(F32)
+        square[...] = jnp.zeros_like(square)
+        for b in range(blocks):
+            square[b : b + 1, :] = targets_ref[0:1, b * LANES : (b + 1) * LANES].astype(F32)
+        square[...] = square[...].T
+
+    tiles = mel_rows // LANES + 2
+
+    def upright(half):
+        if half == 0:
+            for copy in halo:
+                copy.wait_recv()
+
+        @pl.loop(half * (tiles // 2), (half + 1) * (tiles // 2))
+        def _(part):
+            r0 = pl.multiple_of(part * LANES, LANES)
+            past = (z == Z - 1) & (part == tiles - 1)
+            tile = jnp.where(past, 0.0, mel_bf[:, pl.ds(r0, LANES)].astype(F32))
+            mel_f32[pl.ds(r0, LANES), :] = tile.T
+
     tall = wide // 3
+    skip = LANES - 4 * HALO
 
     def stem(part):
         r0 = part * tall
-        window = [mel_f32[pl.ds(4 * r0 + i, tall, stride=4), :] for i in range(8)]
+        window = [mel_f32[pl.ds(skip + 4 * r0 + i, tall, stride=4), :] for i in range(8)]
         frames = jnp.concatenate(window, axis=1).astype(BF16)
         out = dot(frames, stem_w[...]).astype(BF16)
         stem_out[r0 : r0 + tall, :] = out
         normed[r0 : r0 + tall, :] = normalised(out.astype(F32), gain_ref[0, 0:1, :])
-
-    for part in range(3):
-        stem(part)
-        comm(2 + part)
-    comm(5)
-    comm(6)
 
     def gate(group):
         @pl.loop(0, 3)
@@ -299,51 +313,62 @@
                     total = total + partial[:size]
                 swished[pl.ds(r0, size), column : column + LANES] = jax.nn.silu(total).astype(BF16)
 
-    steps = rows // 64
-    gate(0)
-    comm(7)
-    depthwise(0, 0, steps)
-    gate(1)
-    comm(8)
-    depthwise(1, 0, steps)
-    gate(2)
-    comm(9)
-    depthwise(2, 0, steps // 2)
-    comm(10)
-    depthwise(2, steps // 2, steps)
-
-    @pl.loop(0, 16)
-    def _(part):
-        r0 = pl.multiple_of(part * 48, 48)
-        flat_a = back_a.at[part // 4, lax.rem(part // 2, 2), pl.ds(lax.rem(part, 2) * 4, 4)]
-        flat_b = back_b.at[part // 4, lax.rem(part // 2, 2), pl.ds(lax.rem(part, 2) * 4, 4)]
-        back_w[pl.ds(r0, 48), :half] = flat_a[...].astype(F32).reshape(48, half).astype(BF16)
-        back_w[pl.ds(r0, 48), half:] = flat_b[...].astype(F32).reshape(48, half).astype(BF16)
-
-    error_cols[...] = jnp.zeros_like(error_cols)
-    size = 2 * LANES
-    vocab = 2 * quarter
-
-    @pl.loop(0, rows // size)
-    def _(part):
-        r0 = pl.multiple_of(part * size, size)
-        after = stem_out[pl.ds(r0 + HALO, size), :].astype(F32) + dot(swished[pl.ds(r0, size), :], back_w[...])
-        second = normalised(after, gain_ref[0, 1:2, :])
-        logits = jnp.concatenate(
-            [dot(second, head_a[...].reshape(-1, quarter)), dot(second, head_b[...].reshape(-1, quarter))], axis=1
-        )
-        top = jnp.max(logits, axis=-1, keepdims=True)
-        weight = jnp.exp(logits - top)
-        posterior = weight * (1.0 / jnp.sum(weight, axis=-1, keepdims=True))
-        token = lax.broadcasted_iota(jnp.int32, (LANES, vocab), 1).astype(F32)
-        lane = lax.broadcasted_iota(jnp.int32, (LANES, LANES), 1)
-        for k in range(2):
-            here = lane == 2 * part + k
-            target = jnp.sum(jnp.where(here, square[...], 0.0), axis=1, keepdims=True)
-            onehot = jnp.where(token == target, 1.0, 0.0)
-            differ = posterior[k * LANES : (k + 1) * LANES] - onehot
-            norm = jnp.sqrt(jnp.sum(differ * differ, axis=-1, keepdims=True))
-            error_cols[...] = jnp.where(here, norm, error_cols[...])
+    def contiguous():
+        error_cols[...] = jnp.zeros_like(error_cols)
+
+        @pl.loop(0, 16)
+        def _(part):
+            r0 = pl.multiple_of(part * 48, 48)
+            flat_a = back_a.at[part // 4, lax.rem(part // 2, 2), pl.ds(lax.rem(part, 2) * 4, 4)]
+            flat_b = back_b.at[part // 4, lax.rem(part // 2, 2), pl.ds(lax.rem(part, 2) * 4, 4)]
+            back_w[pl.ds(r0, 48), :half] = flat_a[...].astype(F32).reshape(48, half).astype(BF16)
+            back_w[pl.ds(r0, 48), half:] = flat_b[...].astype(F32).reshape(48, half).astype(BF16)
+
+    def scores():
+        size = 2 * LANES
+        vocab = 2 * quarter
+
+        @pl.loop(0, rows // size)
+        def _(part):
+            r0 = pl.multiple_of(part * size, size)
+            after = stem_out[pl.ds(r0 + HALO, size), :].astype(F32) + dot(swished[pl.ds(r0, size), :], back_w[...])
+            second = normalised(after, gain_ref[0, 1:2, :])
+            logits = jnp.concatenate(
+                [dot(second, head_a[...].reshape(-1, quarter)), dot(second, head_b[...].reshape(-1, quarter))], axis=1
+            )
+            top = jnp.max(logits, axis=-1, keepdims=True)
+            weight = jnp.exp(logits - top)
+            posterior = weight * (1.0 / jnp.sum(weight, axis=-1, keepdims=True))
+            token = lax.broadcasted_iota(jnp.int32, (LANES, vocab), 1).astype(F32)
+            lane = lax.broadcasted_iota(jnp.int32, (LANES, LANES), 1)
+            for k in range(2):
+                here = lane == 2 * part + k
+                target = jnp.sum(jnp.where(here, square[...], 0.0), axis=1, keepdims=True)
+                onehot = jnp.where(token == target, 1.0, 0.0)
+                differ = posterior[k * LANES : (k + 1) * LANES] - onehot
+                norm = jnp.sqrt(jnp.sum(differ * differ, axis=-1, keepdims=True))
+                error_cols[...] = jnp.where(here, norm, error_cols[...])
+
+    steps = rows // 64 // 2
+    work = {"misc": small, "reloc": contiguous, "fin": scores}
+    for k in range(2):
+        work["mel%d" % k] = functools.partial(upright, k)
+    for k in range(3):
+        work["stem%d" % k] = functools.partial(stem, k)
+    for k in range(GROUPS):
+        work["gate%d" % k] = functools.partial(gate, k)
+        work["dw%da" % k] = functools.partial(depthwise, k, 0, steps)
+        work["dw%db" % k] = functools.partial(depthwise, k, steps, 2 * steps)
+    sent_halo = False
+    for token in ORDER:
+        if not isinstance(token, int):
+            if not sent_halo:
+                for copy in halo:
+                    copy.start()
+                sent_halo = True
+            work[token]()
+        else:
+            pieces[token].step()
 
     block = lax.broadcasted_iota(jnp.int32, (blocks, LANES), 0)
     position = z * rows + block * LANES + lax.broadcasted_iota(jnp.int32, (blocks, LANES), 1)
@@ -403,21 +428,25 @@
     width = stem_weight.shape[2]
     wide = rows + 2 * HALO
     mels = mel.shape[2]
-    mel_rows = 4 * HALO + mel.shape[1] + TAIL
+    mel_rows = mel.shape[1] + 2 * LANES
     deep, thin = gate_weight.shape[1], back_weight.shape[1]
     vocab = head_weight.shape[2]
     vmem = pl.BlockSpec(memory_space=pltpu.VMEM)
-    hbm = pl.BlockSpec(memory_space=pl.ANY)
+    hbm = pl.BlockSpec(memory_space=pltpu.HBM)
     share = (Y, CORES, Z)
     blocks = rows // LANES
     flops = 2 * wide * width * (stem_weight.shape[1] + 2 * channels) + 2 * rows * width * (channels + vocab)
     error, score = pl.pallas_call(
         functools.partial(kernel, rows, taps),
         out_shape=(jax.ShapeDtypeStruct((1, rows), F32), jax.ShapeDtypeStruct((1, 1), F32)),
-        in_specs=[pl.BlockSpec(memory_space=pltpu.SMEM)] + [vmem] * 4 + [hbm] * 5,
+        in_specs=[pl.BlockSpec(memory_space=pltpu.SMEM)] + [hbm] * 9,
         out_specs=(vmem, vmem),
         scratch_shapes=[
-            pltpu.VMEM((mel_rows, mels), BF16),
+            pltpu.VMEM(targets.shape, jnp.int32),
+            pltpu.VMEM(mask.shape, jnp.int32),
+            pltpu.VMEM(gain.shape, F32),
+            pltpu.VMEM(depth_weight.shape, BF16),
+            pltpu.VMEM((mels, mel_rows), BF16),
             pltpu.VMEM((mel_rows, mels), F32),
             pltpu.VMEM(stem_weight.shape[1:], BF16),
             pltpu.VMEM((GROUPS,) + share + (deep, GROUP), BF16),
@@ -438,18 +467,18 @@
             pltpu.VMEM((Z, blocks, LANES), F32),
             pltpu.SemaphoreType.DMA((10, 11)),
             pltpu.SemaphoreType.DMA((10, 11)),
-            pltpu.SemaphoreType.DMA((12,)),
+            pltpu.SemaphoreType.DMA((16,)),
             pltpu.SemaphoreType.DMA((2,)),
             pltpu.SemaphoreType.DMA((2,)),
             pltpu.SemaphoreType.DMA((X + Z,)),
             pltpu.SemaphoreType.DMA((X + Z,)),
         ],
         compiler_params=pltpu.CompilerParams(
-            collective_id=0, has_side_effects=True, vmem_limit_bytes=52 << 20
+            collective_id=0, has_side_effects=True, vmem_limit_bytes=64 << 20
         ),
         cost_estimate=pl.CostEstimate(flops=flops, bytes_accessed=20 << 20, transcendentals=4 << 20),
         name="el2n_scores",
-    )(lengths, targets, mask, gain, depth_weight, mel, stem_weight, gate_weight, back_weight, head_weight)
+    )(lengths, targets, mask, gain, depth_weight, jnp.swapaxes(mel, 1, 2), stem_weight, gate_weight, back_weight, head_weight)
     return error, score.reshape(1)
 
 

time: 93.5 us -> 78.8 us (0.84)
  Pallas kernels: 82.6 us -> 74.4 us
  local copies, waits for them, and re-layouts: 7.44 us -> 1.26 us
    pallas_call x1, Pallas kernels: 82.6 us -> 74.4 us  [body(): pl.pallas_call(functools.partial(kernel, rows, taps), out_shape=(jax.Shap...]
    unnamed x16 -> x1, local copies, waits for them, and re-layouts: 7.44 us -> 1.26 us
where the time goes in v2:
time: 78.8 us; the launch traced here: 78.7 us
  Pallas kernels  74.4 us (94%)
  between operations  3.05 us (4%)
  local copies, waits for them, and re-layouts  1.26 us (2%)
    pallas_call x1, Pallas kernels, body(): pl.pallas_call(functools.partial(kernel, rows, taps), out_shape=(jax.Shap...  74.4 us

profile of v2, /device:TPU:1, one launch (start us, length us, event | category | flops | bytes accessed | tf_op | source)
XLA Modules:
  0.0 78.7 jit_solution(8229831847474854540)
XLA Ops:
  1.3 74.4 %el2n_scores.1 = (f32[1,1024]{1,0:T(1,128)}, f32[1,1]{1,0:T(1,128)}) custom-call(s32[1]{0:T(128)S(6)} %copy.14.lengths_ref, s32[1,1024]{1,0:T(1,128)} %targets_hbm.1, s32[1,1024]{1,0:T(1,128)} %mask_hbm.1, f32[1,2,1536]{2,1,0:T(2,128)} %gain_hbm.1, bf16[1,31,768]{2,1,0:T(8,128)(2,1)} %depth_hbm.1, bf16[1,80,4096]{2,1,0:T(8,128)(2,1)} %bitcast.2, ...), custom_call_target="tpu_custom_call" | custom-call | flops 11085545472 | bytes 20971520 | tf_op jit(solution)/shard_map/el2n_scores/pallas_call | solution.py:439
  75.7 1.3 %copy.15 = f32[1,1024]{1,0:T(1,128)} copy(f32[1,1024]{1,0:T(1,128)} %get-tuple-element.8) | data formatting | bytes 8192

commit v3 on v2

--- a/solution.py
+++ b/solution.py
@@ -19,7 +19,7 @@
     1, 0, 3, "misc", 4, "mel0", 1, 5, 0, 3, "mel1", 4, "stem0", 1, 2, 5, "stem1", 0, "stem2", 7, 3, 4,
     1, 2, 5, 9, 3, 0, 1, 6, 7, 2, 5, 0, 3, 1, 6, 8, 4, 9, 7, 1, "gate0", 4, 5, 3, "dw0a", 2, 8, 6, "dw0b",
     9, 7, 3, 2, "gate1", 5, 9, 8, "dw1a", 7, "dw1b", 9, 5, 6, "gate2", 7, "dw2a", 9, 8, 6, "dw2b", 7,
-    "reloc", 9, 8, "fin",
+    "reloc", 9, 8, "finA", "finB",
 )
 
 
@@ -186,9 +186,8 @@
     channels = GROUP * GROUPS
 
     barrier = pltpu.get_barrier_semaphore()
-    peers = [(x, fsdp, lax.rem(z + d, Z)) for d in range(1, Z)]
+    peers = [(lax.rem(x + d, X), fsdp, lax.rem(z + e, Z)) for d in range(X) for e in range(Z) if d or e]
     peers += [(x, lax.rem(y + d, Y) * CORES + c, z) for d in range(1, Y)]
-    peers += [(lax.rem(x + d, X), fsdp, z) for d in range(1, X)]
     peers += [(x, y * CORES + 1 - c, z)]
     for peer in peers:
         pl.semaphore_signal(barrier, inc=1, device_id=peer, device_id_type=MESH)
@@ -279,9 +278,8 @@
         normed[r0 : r0 + tall, :] = normalised(out.astype(F32), gain_ref[0, 0:1, :])
 
     def gate(group):
-        @pl.loop(0, 3)
-        def _(part):
-            r0 = pl.multiple_of(part * tall, 16)
+        for part in range(3):
+            r0 = part * tall
             left = normed[pl.ds(r0, tall), :]
             value = dot(left, gate_a[group].reshape(-1, GROUP))
             control = dot(left, gate_b[group].reshape(-1, GROUP))
@@ -292,7 +290,7 @@
                 gated[k, pl.ds(r0, tall), :] = result[:, k * LANES : (k + 1) * LANES]
 
     def depthwise(group, first, last):
-        size = 64
+        size = 128
 
         @pl.loop(first, last)
         def _(part):
@@ -324,33 +322,39 @@
             back_w[pl.ds(r0, 48), :half] = flat_a[...].astype(F32).reshape(48, half).astype(BF16)
             back_w[pl.ds(r0, 48), half:] = flat_b[...].astype(F32).reshape(48, half).astype(BF16)
 
-    def scores():
-        size = 2 * LANES
-        vocab = 2 * quarter
-
+    size = 4 * LANES
+
+    def project():
         @pl.loop(0, rows // size)
         def _(part):
             r0 = pl.multiple_of(part * size, size)
-            after = stem_out[pl.ds(r0 + HALO, size), :].astype(F32) + dot(swished[pl.ds(r0, size), :], back_w[...])
-            second = normalised(after, gain_ref[0, 1:2, :])
+            product = dot(swished[pl.ds(r0, size), :], back_w[...])
+            after = stem_out[pl.ds(r0 + HALO, size), :].astype(F32) + product
+            normed[pl.ds(r0, size), :] = normalised(after, gain_ref[0, 1:2, :])
+
+    def scores():
+        @pl.loop(0, rows // size)
+        def _(part):
+            r0 = pl.multiple_of(part * size, size)
+            second = normed[pl.ds(r0, size), :]
             logits = jnp.concatenate(
                 [dot(second, head_a[...].reshape(-1, quarter)), dot(second, head_b[...].reshape(-1, quarter))], axis=1
             )
             top = jnp.max(logits, axis=-1, keepdims=True)
             weight = jnp.exp(logits - top)
             posterior = weight * (1.0 / jnp.sum(weight, axis=-1, keepdims=True))
-            token = lax.broadcasted_iota(jnp.int32, (LANES, vocab), 1).astype(F32)
+            token = lax.broadcasted_iota(jnp.int32, (LANES, 2 * quarter), 1).astype(F32)
             lane = lax.broadcasted_iota(jnp.int32, (LANES, LANES), 1)
-            for k in range(2):
-                here = lane == 2 * part + k
+            for k in range(size // LANES):
+                here = lane == size // LANES * part + k
                 target = jnp.sum(jnp.where(here, square[...], 0.0), axis=1, keepdims=True)
                 onehot = jnp.where(token == target, 1.0, 0.0)
                 differ = posterior[k * LANES : (k + 1) * LANES] - onehot
                 norm = jnp.sqrt(jnp.sum(differ * differ, axis=-1, keepdims=True))
                 error_cols[...] = jnp.where(here, norm, error_cols[...])
 
-    steps = rows // 64 // 2
-    work = {"misc": small, "reloc": contiguous, "fin": scores}
+    steps = rows // 128 // 2
+    work = {"misc": small, "reloc": contiguous, "finA": project, "finB": scores}
     for k in range(2):
         work["mel%d" % k] = functools.partial(upright, k)
     for k in range(3):
@@ -376,44 +380,36 @@
         square[b : b + 1, :] = mask_ref[0:1, b * LANES : (b + 1) * LANES].astype(F32)
     own = error_cols[...].T[:blocks] * jnp.where(position < length, 1.0, 0.0) * square[:blocks, :]
     seed_parts[x] = own
-    sums = [
+    seq_parts[x, z] = jnp.sum(own, axis=0, keepdims=True)
+    copies = []
+    for d in range(1, X):
+        copies.append((seed_parts.at[x], (lax.rem(x + d, X), fsdp, z)))
+    for e in (4, 3, 5, 2, 6, 1, 7, 0):
+        for d in (2, 1, 3, 0):
+            if d or e:
+                copies.append((seq_parts.at[x, z], (lax.rem(x + d, X), fsdp, lax.rem(z + e, Z))))
+    copies = [
         pltpu.make_async_remote_copy(
-            src_ref=seed_parts.at[x],
-            dst_ref=seed_parts.at[x],
-            send_sem=out_send.at[d],
-            recv_sem=out_recv.at[d],
-            device_id=(lax.rem(x + d, X), fsdp, z),
+            src_ref=ref,
+            dst_ref=ref,
+            send_sem=out_send.at[k],
+            recv_sem=out_recv.at[k],
+            device_id=device,
             device_id_type=MESH,
         )
-        for d in range(1, X)
+        for k, (ref, device) in enumerate(copies)
     ]
-    for copy in sums:
+    for copy in copies:
         copy.start()
-    for copy in sums:
+    for copy in copies[: X - 1]:
         copy.wait()
     frame_error = (seed_parts[0] + seed_parts[1] + seed_parts[2] + seed_parts[3]) / 4.0
     for b in range(blocks):
         error_ref[0:1, b * LANES : (b + 1) * LANES] = frame_error[b : b + 1]
-    seq_parts[z] = frame_error
-    shares = [
-        pltpu.make_async_remote_copy(
-            src_ref=seq_parts.at[z],
-            dst_ref=seq_parts.at[z],
-            send_sem=out_send.at[X + d],
-            recv_sem=out_recv.at[X + d],
-            device_id=(x, fsdp, lax.rem(z + d, Z)),
-            device_id_type=MESH,
-        )
-        for d in range(1, Z)
-    ]
-    for copy in shares:
-        copy.start()
-    for copy in shares:
+    for copy in copies[X - 1 :]:
         copy.wait()
-    total = seq_parts[0]
-    for k in range(1, Z):
-        total = total + seq_parts[k]
-    numerator = jnp.sum(jnp.sum(total, axis=1, keepdims=True), axis=0, keepdims=True)
+    total = jnp.sum(seq_parts[...].reshape(X * Z, LANES), axis=0, keepdims=True) / 4.0
+    numerator = jnp.sum(total, axis=1, keepdims=True)
     score_ref[...] = numerator / jnp.full((1, 1), length, jnp.int32).astype(F32)
 
     for copy in halo:
@@ -464,14 +460,14 @@
             pltpu.VMEM((LANES, LANES), F32),
             pltpu.VMEM((LANES, LANES), F32),
             pltpu.VMEM((X, blocks, LANES), F32),
-            pltpu.VMEM((Z, blocks, LANES), F32),
+            pltpu.VMEM((X, Z, 1, LANES), F32),
             pltpu.SemaphoreType.DMA((10, 11)),
             pltpu.SemaphoreType.DMA((10, 11)),
             pltpu.SemaphoreType.DMA((16,)),
             pltpu.SemaphoreType.DMA((2,)),
             pltpu.SemaphoreType.DMA((2,)),
-            pltpu.SemaphoreType.DMA((X + Z,)),
-            pltpu.SemaphoreType.DMA((X + Z,)),
+            pltpu.SemaphoreType.DMA((X - 1 + X * Z - 1,)),
+            pltpu.SemaphoreType.DMA((X - 1 + X * Z - 1,)),
         ],
         compiler_params=pltpu.CompilerParams(
             collective_id=0, has_side_effects=True, vmem_limit_bytes=64 << 20

time: 78.8 us -> 77.5 us (0.984)
  Pallas kernels: 74.4 us -> 73 us
    pallas_call x1, Pallas kernels: 74.4 us -> 73 us  [body(): pl.pallas_call(functools.partial(kernel, rows, taps), out_shape=(jax.Shap...]
where the time goes in v3:
time: 77.5 us; the launch traced here: 77.3 us
  Pallas kernels  73 us (94%)
  between operations  3.05 us (4%)
  local copies, waits for them, and re-layouts  1.26 us (2%)
    pallas_call x1, Pallas kernels, body(): pl.pallas_call(functools.partial(kernel, rows, taps), out_shape=(jax.Shap...  73 us

profile of v3, /device:TPU:1, one launch (start us, length us, event | category | flops | bytes accessed | tf_op | source)
XLA Modules:
  0.0 77.3 jit_solution(2277688611444548750)
XLA Ops:
  1.3 73.0 %el2n_scores.1 = (f32[1,1024]{1,0:T(1,128)}, f32[1,1]{1,0:T(1,128)}) custom-call(s32[1]{0:T(128)S(6)} %copy.14.lengths_ref, s32[1,1024]{1,0:T(1,128)} %targets_hbm.1, s32[1,1024]{1,0:T(1,128)} %mask_hbm.1, f32[1,2,1536]{2,1,0:T(2,128)} %gain_hbm.1, bf16[1,31,768]{2,1,0:T(8,128)(2,1)} %depth_hbm.1, bf16[1,80,4096]{2,1,0:T(8,128)(2,1)} %bitcast.2, ...), custom_call_target="tpu_custom_call" | custom-call | flops 11085545472 | bytes 20971520 | tf_op jit(solution)/shard_map/el2n_scores/pallas_call | solution.py:435
  74.3 1.3 %copy.15 = f32[1,1024]{1,0:T(1,128)} copy(f32[1,1024]{1,0:T(1,128)} %get-tuple-element.8) | data formatting | bytes 8192

commit v4 on v3

--- a/solution.py
+++ b/solution.py
@@ -16,10 +16,10 @@
 GROUPS = 3
 Y, CORES, Z, X = 4, 2, 8, 4
 ORDER = (
-    1, 0, 3, "misc", 4, "mel0", 1, 5, 0, 3, "mel1", 4, "stem0", 1, 2, 5, "stem1", 0, "stem2", 7, 3, 4,
-    1, 2, 5, 9, 3, 0, 1, 6, 7, 2, 5, 0, 3, 1, 6, 8, 4, 9, 7, 1, "gate0", 4, 5, 3, "dw0a", 2, 8, 6, "dw0b",
-    9, 7, 3, 2, "gate1", 5, 9, 8, "dw1a", 7, "dw1b", 9, 5, 6, "gate2", 7, "dw2a", 9, 8, 6, "dw2b", 7,
-    "reloc", 9, 8, "finA", "finB",
+    1, 2, 0, "misc", 4, "mel0", 1, 2, 3, "mel1", 5, 0, 4, "stem0", 1, 3, "stem1", 2, "stem2", 5, 7, 6,
+    0, 4, 9, 1, 3, 5, 6, 2, 1, 7, 3, 8, 5, 2, 1, 6, 0, 7, 3, 1, 8, 0, "gate0", 5, 9, 4, "dw0a", 3, 7,
+    8, "dw0b", 5, 4, 9, 3, "gate1", 5, 7, 6, "dw1a", 9, "dw1b", "gate2", 7, 8, 6, 9, "dw2a", "dw2b", 7,
+    "reloc", 9, "finA", 8, 9, "finB",
 )
 
 

time: 77.5 us -> 77.9 us (level)
  no operation moved by 1% of the time
where the time goes in v4:
time: 77.9 us; the launch traced here: 77.8 us
  Pallas kernels  73.4 us (94%)
  between operations  3.05 us (4%)
  local copies, waits for them, and re-layouts  1.26 us (2%)
    pallas_call x1, Pallas kernels, body(): pl.pallas_call(functools.partial(kernel, rows, taps), out_shape=(jax.Shap...  73.4 us

profile of v4, /device:TPU:1, one launch (start us, length us, event | category | flops | bytes accessed | tf_op | source)
XLA Modules:
  0.0 77.8 jit_solution(11174262817688933822)
XLA Ops:
  1.3 73.4 %el2n_scores.1 = (f32[1,1024]{1,0:T(1,128)}, f32[1,1]{1,0:T(1,128)}) custom-call(s32[1]{0:T(128)S(6)} %copy.14.lengths_ref, s32[1,1024]{1,0:T(1,128)} %targets_hbm.1, s32[1,1024]{1,0:T(1,128)} %mask_hbm.1, f32[1,2,1536]{2,1,0:T(2,128)} %gain_hbm.1, bf16[1,31,768]{2,1,0:T(8,128)(2,1)} %depth_hbm.1, bf16[1,80,4096]{2,1,0:T(8,128)(2,1)} %bitcast.2, ...), custom_call_target="tpu_custom_call" | custom-call | flops 11085545472 | bytes 20971520 | tf_op jit(solution)/shard_map/el2n_scores/pallas_call | solution.py:435
  74.7 1.3 %copy.15 = f32[1,1024]{1,0:T(1,128)} copy(f32[1,1024]{1,0:T(1,128)} %get-tuple-element.8) | data formatting | bytes 8192
